TPU v7x, 512 devices: a whole 4x4x16 slice. The times are simulated.
512 devices in a mesh: src: 8 (over y_hi, x), space: 64 (over z, y_lo, core).
Axes of the slice: x: 4, y: 4 (y_hi: 2, y_lo: 2; y = y_hi * 2 + y_lo), z: 16, core: 2. Of those that a mesh axis runs over, the one named last changes fastest.
Arguments:
- propagators: bfloat16 [64, 2, 144, 8192], P('src', None, None, 'space'), may hold values from -1.5 to 1.5
- source_coords: int32 [64, 3], replicated, may hold values from 0 to 95
- momenta: int32 [33, 3], replicated, may hold values from -2 to 2
- slab_start: int32 [1], replicated, may hold values from 0 to 884735
Outputs:
- correlator: float32 [64, 64, 2, 33], P('src', 'space')
All inputs are finite; a program needn't handle non-finite values.
Results may differ from a plain program's by a relative error of at most 0.0026.
Values may be sent and summed in bfloat16 or wider, within the bound.
A program may use at most 64 MiB of HBM per device.

v0:
```python
import math

import jax
import jax.numpy as jnp
from jax import lax
from jax.sharding import PartitionSpec as P

LAT = 96


def phase_table(site_index, momenta):
    cube = LAT * LAT * LAT
    glob = jnp.mod(site_index, cube)
    first = glob // (LAT * LAT)
    second = jnp.mod(glob // LAT, LAT)
    third = jnp.mod(glob, LAT)
    dotted = (
        first[:, None] * momenta[None, :, 0]
        + second[:, None] * momenta[None, :, 1]
        + third[:, None] * momenta[None, :, 2]
    )
    angle = jnp.mod(dotted, LAT).astype(jnp.float32) * jnp.float32(2.0 * math.pi / LAT)
    return jnp.concatenate([jnp.cos(angle), jnp.sin(angle)], axis=1).astype(jnp.bfloat16)


def pair_traces(left, right):
    count_a = left.shape[0]
    count_b = right.shape[0]
    width = left.shape[3]
    real_part = jnp.einsum(
        "akx,bkx->abx",
        left.reshape(count_a, -1, width),
        right.reshape(count_b, -1, width),
        preferred_element_type=jnp.float32,
    )
    imag_part = jnp.einsum(
        "acx,bcx->abx", left[:, 0], right[:, 1], preferred_element_type=jnp.float32
    ) - jnp.einsum("acx,bcx->abx", left[:, 1], right[:, 0], preferred_element_type=jnp.float32)
    return jnp.stack([real_part, imag_part], axis=2).astype(jnp.bfloat16)


def project(pair_trace, phases):
    count_a, count_b, two, width = pair_trace.shape
    moms = phases.shape[1] // 2
    prod = jnp.dot(pair_trace.reshape(-1, width), phases, preferred_element_type=jnp.float32)
    prod = prod.reshape(count_a, count_b, 2, 2, moms)
    real_part = prod[:, :, 0, 0] + prod[:, :, 1, 1]
    imag_part = prod[:, :, 1, 0] - prod[:, :, 0, 1]
    return jnp.stack([real_part, imag_part], axis=2)


def finish(raw, coords, momenta, total_sites):
    dotted = jnp.mod(coords @ momenta.T, LAT)
    angle = dotted.astype(jnp.float32) * jnp.float32(2.0 * math.pi / LAT)
    cosine = jnp.cos(angle)[None, :, :]
    sine = jnp.sin(angle)[None, :, :]
    real_part = raw[:, :, 0]
    imag_part = raw[:, :, 1]
    scale = jnp.float32(1.0 / math.sqrt(total_sites))
    new_real = (real_part * cosine - imag_part * sine) * scale
    new_imag = (real_part * sine + imag_part * cosine) * scale
    return jnp.stack([new_real, new_imag], axis=2)


def per_device(propagators, source_coords, momenta, slab_start):
    src_count = lax.axis_size("src")
    space_count = lax.axis_size("space")
    local_src = propagators.shape[0]
    local_sites = propagators.shape[3]
    total_src = local_src * src_count
    total_sites = local_sites * space_count
    space_pos = lax.axis_index("space")
    block_b = total_src // space_count
    site_index = slab_start[0] + space_pos * local_sites + jnp.arange(local_sites, dtype=jnp.int32)
    phases = phase_table(site_index, momenta)
    partial_value = project(
        pair_traces(propagators, lax.all_gather(propagators, "src", axis=0, tiled=True)), phases
    )
    summed = lax.psum_scatter(partial_value, "space", scatter_dimension=1, tiled=True)
    coords_b = lax.dynamic_slice_in_dim(source_coords, space_pos * block_b, block_b, 0)
    return finish(summed, coords_b, momenta, total_sites)


def solution(mesh):
    placed = (P("src", None, None, "space"), P(), P(), P())
    return jax.shard_map(
        per_device,
        mesh=mesh,
        in_specs=placed,
        out_specs=P("src", "space", None, None),
        check_vma=False,
    )
```

profile of v0, /device:TPU:1, one launch (start us, length us, event | category | flops | bytes accessed | tf_op | source)
XLA Modules:
  0.0 415.8 jit_solution(16339691402150731810)
XLA Ops:
  6.5 0.0 copy-start
  6.5 0.0 all-gather.2.cloned.1.call-start
  6.5 2.6 copy.24
  9.1 0.0 all-gather.2.cloned.1.call-update
  9.1 0.0 reduce-scatter.2.cloned.1.call-start
  9.2 1.6 copy.27
  11.5 0.8 slice_bitcast_fusion.18
  12.3 0.2 cosine_convert_fusion
  12.5 138.3 %all-gather.2.cloned.1.call-done = bf16[64,2,144,128]{2,0,3,1:T(8,128)(2,1)} async-done(((bf16[8,2,144,128]{2,0,3,1:T(8,128)(2,1)}), bf16[64,2,144,128]{2,0,3,1:T(8,128)(2,1)}) %all-gather.2.cloned.1.call-update) | async-done | bytes 4718608 | tf_op jit(solution)/shard_map/all_gather | solution.py:77
  150.8 12.0 %copy.25 = bf16[64,2,144,128]{3,2,1,0:T(8,128)(2,1)} copy(bf16[64,2,144,128]{2,0,3,1:T(8,128)(2,1)} %all-gather.2.cloned.1.call-done) | data formatting | bytes 9437184 | tf_op jit(solution)/shard_map/all_gather | solution.py:77
  162.8 8.6 %copy.26 = bf16[64,288,128]{1,0,2:T(8,128)(2,1)} copy(bf16[64,288,128]{2,1,0:T(8,128)(2,1)} %bitcast.75) | data formatting | bytes 9437184 | tf_op jit(solution)/shard_map/reshape | solution.py:33
  171.4 0.0 copy-start.1
  171.4 5.1 %fusion.4 = bf16[8,64,1,128]{1,0,3,2:T(8,128)(2,1)S(1)} fusion(bf16[64,288,128]{1,0,2:T(8,128)(2,1)} %copy.26, bf16[8,288,128]{1,0,2:T(8,128)(2,1)S(1)} %copy.27), kind=kOutput, calls=%fused_computation.7 | convolution fusion | flops 37814272 | bytes 5439488 | tf_op jit(solution)/shard_map/akx,bkx->abx/dot_general | solution.py:30
  176.6 0.0 copy-done.1
  176.6 3.4 fusion
  179.9 0.0 copy-start.2
  179.9 3.4 fusion.5
  183.3 0.1 maximum_bitcast_fusion
  183.5 0.2 fusion.7
  183.8 1.1 copy.33
  184.9 0.0 reduce-scatter.2.cloned.1.call-update
  184.9 0.0 copy-done
  184.9 0.2 dynamic-slice_reduce_fusion
  185.1 0.0 copy-done.2
  185.1 0.2 fusion.21
  185.3 222.4 %reduce-scatter.2.cloned.1.call-done = f32[8,1,2,33]{3,0,2,1:T(8,128)} async-done(((f32[8,64,2,33]{3,0,2,1:T(8,128)}), f32[8,1,2,33]{3,0,2,1:T(8,128)}) %reduce-scatter.2.cloned.1.call-update) | async-done | bytes 2128 | tf_op jit(solution)/shard_map/reduce_scatter | solution.py:79
  407.7 0.7 subtract_multiply_fusion
  408.4 0.6 copy.34
  (8 shorter events, 0.2 us)
Async XLA Ops:
  6.5 178.4 %copy-start = (s32[64,3]{0,1:T(4,128)S(1)}, s32[64,3]{0,1:T(4,128)}, u32[]{:S(2)}) copy-start(s32[64,3]{0,1:T(4,128)} %param.5) | copy-start | bytes 2308
  6.5 144.3 %all-gather.2.cloned.1.call-start = ((), (), s32[]{:S(2)}) async-start(), calls=%async_computation.1 | async-start | bytes 9437184 | tf_op jit(solution)/shard_map/all_gather | solution.py:77
  9.1 398.5 %reduce-scatter.2.cloned.1.call-start = ((), (), s32[]{:S(2)}) async-start(), calls=%async_computation.2 | async-start | bytes 532480 | tf_op jit(solution)/shard_map/reduce_scatter | solution.py:79
  171.4 5.2 %copy-start.1 = (bf16[8,2,144,128]{2,0,3,1:T(8,128)(2,1)S(1)}, bf16[8,2,144,128]{2,0,3,1:T(8,128)(2,1)}, u32[]{:S(2)}) copy-start(bf16[8,2,144,128]{2,0,3,1:T(8,128)(2,1)} %copy.24) | copy-start | bytes 1769476
  179.9 5.2 %copy-start.2 = (s32[33,3]{0,1:T(4,128)S(1)}, s32[33,3]{0,1:T(4,128)}, u32[]{:S(2)}) copy-start(s32[33,3]{0,1:T(4,128)} %param.6) | copy-start | bytes 1192
Sparse Core Ops, SparseCore 0:
  10.4 140.3 all-gather.1
  185.1 222.5 reduce-scatter.1
where the time goes:
time: 419 us; the launch traced here: 416 us
  waiting for transfers between devices  361 us (86%)
  local copies, waits for them, and re-layouts  27.4 us (7%)
  between operations  14.1 us (3%)
  matrix products  12.4 us (3%)
    reduce_scatter x1, waiting for transfers between devices, per_device(): lax.psum_scatter(partial_value, 'space', scatter_dimension=1, tiled=True)  222 us
    all_gather x1, waiting for transfers between devices, per_device(): lax.all_gather(propagators, 'src', axis=0, tiled=True)  138 us
    all_gather x1, local copies, waits for them, and re-layouts, per_device(): lax.all_gather(propagators, 'src', axis=0, tiled=True)  12 us
    reshape x1, local copies, waits for them, and re-layouts, pair_traces(): right.reshape(count_b, -1, width)  8.59 us
  transfers between devices with their start and end apart: 2, of which 2 were waited for; matrix products, arithmetic and copies ran while one was open for 1% of the time, Pallas kernels for 0%

commit v1 on v0

v1 whole, which is shorter than its diff:
```python
import functools
import math

import jax
import jax.numpy as jnp
from jax import lax
from jax.experimental import pallas as pl
from jax.experimental.pallas import tpu as pltpu
from jax.sharding import PartitionSpec as P

LAT = 96
NC2 = 144
K = 2 * NC2
NMOM = 33
NSRC_AX = 8
NQ = 4
NZ = 16
LANES = 128
MESH = pl.DeviceIdType.MESH
BF = jnp.bfloat16
F32 = jnp.float32


def swap_bits(vs, bits, lane):
    vs = list(vs)
    for bit, s in bits:
        low = (lane & s) == 0
        for u in range(len(vs)):
            if u & bit:
                continue
            a, b = vs[u], vs[u | bit]
            vs[u] = jnp.where(low, a, pltpu.roll(b, s, 1))
            vs[u | bit] = jnp.where(low, pltpu.roll(a, LANES - s, 1), b)
    return vs


def mod_lat(u):
    return u - LAT * jnp.floor((u + 0.5) * (1.0 / LAT))


def cos_steps(u):
    t = (jnp.abs(u - 48.0) - 24.0) * (2.0 * math.pi / LAT)
    t2 = t * t
    acc = jnp.full_like(t, 1.0 / math.factorial(13))
    for n in (11, 9, 7, 5, 3, 1):
        sign = 1.0 if n % 4 == 1 else -1.0
        acc = acc * t2 + sign / math.factorial(n)
    return acc * t


def kernel(
    prop, coords, momenta, slab, out,
    x_in, send1, recv1, lt, tt, gram, send2, recv2, lhs, wts, send3, recv3,
    in_sem, loc_sem, s1, r1, s2, r2, s3, r3,
):
    src = lax.axis_index("src")
    space = lax.axis_index("space")
    z = space // NQ
    q = space % NQ
    sx = src % 4
    sy = src // 4

    load = pltpu.make_async_copy(prop, x_in, in_sem)
    load.start()

    barrier = pltpu.get_barrier_semaphore()
    for r in range(1, NSRC_AX * NQ):
        dev = {"src": (src + r // NQ) % NSRC_AX, "space": z * NQ + (q + r) % NQ}
        pl.semaphore_signal(barrier, inc=1, device_id=dev, device_id_type=MESH)
    for r in range(1, NZ):
        dev = {"src": src, "space": ((z + r) % NZ) * NQ + q}
        pl.semaphore_signal(barrier, inc=1, device_id=dev, device_id_type=MESH)

    load.wait()
    lane16 = lax.broadcasted_iota(jnp.int32, (16, LANES), 1)
    for c in range(2):
        for t in range(NC2 // 16):
            vs = [x_in[b, c, t * 16 : t * 16 + 16, :] for b in range(8)]
            vs = swap_bits(vs, ((1, 1), (2, 2), (4, 4)), lane16)
            for d in range(8):
                row = c * NC2 + t * 16
                send1[d, row : row + 16, :] = vs[d]

    pl.semaphore_wait(barrier, NSRC_AX * NQ - 1 + NZ - 1)

    order = ((0, 1), (0, 3), (1, 0), (0, 2), (1, 1), (1, 3), (1, 2))
    own = pltpu.make_async_copy(send1.at[src], recv1.at[src], loc_sem.at[0])
    own.start()
    out1 = []
    for dy, dx in order:
        d = ((sy + dy) % 2) * 4 + (sx + dx) % 4
        cp = pltpu.make_async_remote_copy(
            src_ref=send1.at[d], dst_ref=recv1.at[src], send_sem=s1.at[d], recv_sem=r1.at[src],
            device_id={"src": d, "space": space}, device_id_type=MESH,
        )
        cp.start()
        out1.append(cp)

    lane1 = lax.broadcasted_iota(jnp.int32, (1, LANES), 1)
    first_half = lane1 < NMOM
    m3 = momenta[...].astype(F32)
    m3 = jnp.concatenate([m3, m3, jnp.zeros((3, LANES - 2 * NMOM), F32)], axis=1)
    base = slab[0] + z * (NQ * LANES)
    shift_a = jnp.where(first_half, 0.0, 24.0)
    shift_b = jnp.where(first_half, 72.0, 0.0)
    rows = 64

    def phases(step, carry):
        site = lax.broadcasted_iota(jnp.int32, (rows, LANES), 0) + (base + step * rows)
        site = jnp.where(site >= LAT * LAT * LAT, site - LAT * LAT * LAT, site).astype(F32)
        x0 = jnp.floor((site + 0.5) * (1.0 / (LAT * LAT)))
        rest = site - x0 * (LAT * LAT)
        x1 = jnp.floor((rest + 0.5) * (1.0 / LAT))
        x2 = rest - x1 * LAT
        u = x0 * m3[0:1] + x1 * m3[1:2] + x2 * m3[2:3]
        w = jnp.concatenate([cos_steps(mod_lat(u + shift_a)), cos_steps(mod_lat(u + shift_b))], axis=1)
        wts[pl.ds(pl.multiple_of(step * rows, rows), rows), :] = w.astype(BF)
        return carry

    lax.fori_loop(0, NQ * LANES // rows, phases, 0)

    def take(j):
        block = recv1[j]
        lt[pl.ds(pl.multiple_of(j * LANES, LANES), LANES), :] = block.T

    own.wait()
    take(src)
    for dy, dx in order:
        d = ((sy - dy + 2) % 2) * 4 + (sx - dx + 4) % 4
        pltpu.make_async_remote_copy(
            src_ref=send1.at[d], dst_ref=recv1.at[d], send_sem=s1.at[d], recv_sem=r1.at[d],
            device_id={"src": d, "space": space}, device_id_type=MESH,
        ).wait_recv()
        take(d)

    lane8 = lax.broadcasted_iota(jnp.int32, (8, LANES), 1) >> 3
    picks = [lane8 == x for x in range(16)]

    def columns(j, carry):
        block = recv1[j]
        turned = jnp.concatenate([block[NC2:], -block[:NC2]], axis=0)
        w = jnp.concatenate([block, turned], axis=1)
        tt[...] = jnp.dot(lt[...], w, preferred_element_type=F32)

        def pick(i, carry2):
            at = pl.multiple_of(i * LANES, LANES)
            parts = []
            for c in range(2):
                acc = jnp.zeros((8, LANES), F32)
                for x in range(16):
                    acc = jnp.where(picks[x], tt[pl.ds(at + 8 * x, 8), c * LANES : (c + 1) * LANES], acc)
                parts.append(acc)
            gram[i, j] = jnp.concatenate(parts, axis=0).astype(BF)
            return carry2

        lax.fori_loop(0, 8, pick, 0)
        return carry

    lax.fori_loop(0, 8, columns, 0)

    def split(i, carry):
        for jhi in range(2):
            vs = [gram[i, 4 * jhi + jlo] for jlo in range(4)]
            vs = swap_bits(vs, ((1, 1), (2, 2)), lane16)
            for t in range(4):
                send2[i * NQ + t, jhi * 16 : jhi * 16 + 16, :] = vs[t]
        return carry

    lax.fori_loop(0, 8, split, 0)

    me = src * NQ + q
    own2 = pltpu.make_async_copy(send2.at[me], recv2.at[me], loc_sem.at[1])
    own2.start()
    out2 = []
    for r in range(1, NSRC_AX * NQ):
        ds, dq = (src + r // NQ) % NSRC_AX, (q + r) % NQ
        to = ds * NQ + dq
        cp = pltpu.make_async_remote_copy(
            src_ref=send2.at[to], dst_ref=recv2.at[me], send_sem=s2.at[to], recv_sem=r2.at[me],
            device_id={"src": ds, "space": z * NQ + dq}, device_id_type=MESH,
        )
        cp.start()
        out2.append(cp)
    own2.wait()
    for r in range(1, NSRC_AX * NQ):
        ds, dq = (src - r // NQ + NSRC_AX) % NSRC_AX, (q - r % NQ + NQ) % NQ
        at = ds * NQ + dq
        pltpu.make_async_remote_copy(
            src_ref=send2.at[at], dst_ref=recv2.at[at], send_sem=s2.at[at], recv_sem=r2.at[at],
            device_id={"src": ds, "space": z * NQ + dq}, device_id_type=MESH,
        ).wait_recv()

    for qq in range(NQ):
        for jhi in range(2):
            vs = [recv2[d * NQ + qq, jhi * 16 : jhi * 16 + 16, :] for d in range(8)]
            vs = swap_bits(vs, ((1, 1), (2, 2), (4, 4)), lane16)
            for b in range(8):
                row = (jhi * 8 + b) * 16
                lhs[row : row + 16, qq * LANES : (qq + 1) * LANES] = vs[b]
    prod = jnp.dot(lhs[...], wts[...], preferred_element_type=F32)
    for b in range(16):
        zb = 8 * (b // 8) + 2 * (b % 4) + (b // 4) % 2
        send3[zb] = prod[b * 16 : b * 16 + 8, :LANES] + prod[b * 16 + 8 : b * 16 + 16, LANES:]

    own3 = pltpu.make_async_copy(send3.at[z], recv3.at[z], loc_sem.at[2])
    own3.start()
    out3 = []
    for r in range(1, NZ):
        to = (z + r) % NZ
        cp = pltpu.make_async_remote_copy(
            src_ref=send3.at[to], dst_ref=recv3.at[z], send_sem=s3.at[to], recv_sem=r3.at[z],
            device_id={"src": src, "space": to * NQ + q}, device_id_type=MESH,
        )
        cp.start()
        out3.append(cp)
    own3.wait()
    for r in range(1, NZ):
        at = (z - r + NZ) % NZ
        pltpu.make_async_remote_copy(
            src_ref=send3.at[at], dst_ref=recv3.at[at], send_sem=s3.at[at], recv_sem=r3.at[at],
            device_id={"src": src, "space": at * NQ + q}, device_id_type=MESH,
        ).wait_recv()
    total = recv3[0]
    for t in range(1, NZ):
        total = total + recv3[t]

    here = lax.broadcasted_iota(jnp.int32, (3, 64), 1) == space
    xyz = jnp.sum(jnp.where(here, coords[...].astype(F32), 0.0), axis=1, keepdims=True)
    u = jnp.sum(xyz * m3, axis=0, keepdims=True)
    scale = 1.0 / math.sqrt(NZ * NQ * LANES)
    cosine = cos_steps(mod_lat(u)) * scale
    sine = cos_steps(mod_lat(u + jnp.where(first_half, 24.0, 72.0))) * scale
    swapped = jnp.where(first_half, pltpu.roll(total, LANES - NMOM, 1), pltpu.roll(total, NMOM, 1))
    done = total * cosine + swapped * sine
    out[0, 0] = done[:, :NMOM]
    out[0, 1] = pltpu.roll(done, LANES - NMOM, 1)[:, :NMOM]

    for cp in out1 + out2 + out3:
        cp.wait_send()


def per_device(propagators, source_coords, momenta, slab_start):
    vm = pl.BlockSpec(memory_space=pltpu.VMEM)
    dma = pltpu.SemaphoreType.DMA
    result = pl.pallas_call(
        kernel,
        out_shape=jax.ShapeDtypeStruct((1, 2, 8, NMOM), F32),
        in_specs=[pl.BlockSpec(memory_space=pl.ANY), vm, vm, pl.BlockSpec(memory_space=pltpu.SMEM)],
        out_specs=vm,
        scratch_shapes=[
            pltpu.VMEM((8, 2, NC2, LANES), BF),
            pltpu.VMEM((8, K, LANES), BF),
            pltpu.VMEM((8, K, LANES), BF),
            pltpu.VMEM((8 * LANES, K), BF),
            pltpu.VMEM((8 * LANES, 2 * LANES), F32),
            pltpu.VMEM((8, 8, 16, LANES), BF),
            pltpu.VMEM((32, 32, LANES), BF),
            pltpu.VMEM((32, 32, LANES), BF),
            pltpu.VMEM((256, NQ * LANES), BF),
            pltpu.VMEM((NQ * LANES, 2 * LANES), BF),
            pltpu.VMEM((NZ, 8, LANES), F32),
            pltpu.VMEM((NZ, 8, LANES), F32),
            dma,
            dma((3,)),
            dma((8,)),
            dma((8,)),
            dma((32,)),
            dma((32,)),
            dma((16,)),
            dma((16,)),
        ],
        compiler_params=pltpu.CompilerParams(
            collective_id=0, has_side_effects=True, vmem_limit_bytes=32 * 1024 * 1024
        ),
    )(propagators, source_coords.T, momenta.T, slab_start)
    return jnp.transpose(result, (2, 0, 1, 3))


def solution(mesh):
    placed = (P("src", None, None, "space"), P(), P(), P())
    return jax.shard_map(
        per_device,
        mesh=mesh,
        in_specs=placed,
        out_specs=P("src", "space", None, None),
        check_vma=False,
    )
```

time: 419 us -> 49.6 us (0.12)
  waiting for transfers between devices: 361 us -> 0 us
  Pallas kernels: 0 us -> 46.2 us
  local copies, waits for them, and re-layouts: 27.4 us -> 2.34 us
  between operations: 14.1 us -> 0.69 us
  matrix products: 12.4 us -> 0 us
    reduce_scatter x1 -> x0, waiting for transfers between devices: 222 us -> none  [per_device(): lax.psum_scatter(partial_value, 'space', scatter_dimension=1, tiled=True)]
    all_gather x1 -> x0, waiting for transfers between devices: 138 us -> none  [per_device(): lax.all_gather(propagators, 'src', axis=0, tiled=True)]
    pallas_call x0 -> x1, Pallas kernels: none -> 46.2 us  [per_device(): pl.pallas_call(kernel, out_shape=jax.ShapeDtypeStruct((1, 2, 8, NMOM), F3...]
    dot_general x5 -> x0, matrix products: 12.4 us -> none  [the longest x1 5.15 us: pair_traces(): jnp.einsum('akx,bkx->abx', left.reshape(count_a, -1, width), right.reshap...]
    all_gather x1 -> x0, local copies, waits for them, and re-layouts: 12 us -> none  [per_device(): lax.all_gather(propagators, 'src', axis=0, tiled=True)]
    reshape x2 -> x0, local copies, waits for them, and re-layouts: 10.2 us -> none  [the longest x1 8.59 us: pair_traces(): right.reshape(count_b, -1, width)]
  transfers between devices with their start and end apart: 2 -> 0, of which waited for: 2 -> 0; matrix products, arithmetic and copies ran while one was open for 1% -> 0% of each run, Pallas kernels for 0% -> 0%
where the time goes in v1:
time: 49.6 us; the launch traced here: 49.3 us
  Pallas kernels  46.2 us (93%)
  local copies, waits for them, and re-layouts  2.34 us (5%)
  between operations  0.69 us (1%)
    pallas_call x1, Pallas kernels, per_device(): pl.pallas_call(kernel, out_shape=jax.ShapeDtypeStruct((1, 2, 8, NMOM), F3...  46.2 us
    unnamed x6, local copies, waits for them, and re-layouts  1.73 us

profile of v1, /device:TPU:1, one launch (start us, length us, event | category | flops | bytes accessed | tf_op | source)
XLA Modules:
  0.0 49.3 jit_solution(111092583812660543)
XLA Ops:
  0.0 0.0 copy-start.2
  0.7 0.0 copy-start.1
  0.7 0.0 copy-done.2
  0.7 0.7 %copy-done.1 = s32[64,3]{0,1:T(4,128)S(1)} copy-done((s32[64,3]{0,1:T(4,128)S(1)}, s32[64,3]{0,1:T(4,128)}, u32[]{:S(2)}) %copy-start.1) | copy-done | bytes 792
  1.4 0.0 copy-start
  1.4 1.1 %copy-done = bf16[8,2,144,128]{3,2,1,0:T(8,128)(2,1)S(1)} copy-done((bf16[8,2,144,128]{3,2,1,0:T(8,128)(2,1)S(1)}, bf16[8,2,144,128]{3,2,1,0:T(8,128)(2,1)}, u32[]{:S(2)}) %copy-start) | copy-done | bytes 589848
  2.4 46.2 %shard_map.46 = f32[1,2,8,33]{3,2,1,0:T(8,128)S(1)} custom-call(bf16[8,2,144,128]{3,2,1,0:T(8,128)(2,1)S(1)} %copy-done, s32[3,64]{1,0:T(4,128)S(1)} %bitcast.4, s32[3,33]{1,0:T(4,128)S(1)} %bitcast.5, s32[1]{0:T(128)S(6)} %copy.6.slab), custom_call_target="tpu_custom_call" | custom-call | tf_op jit(solution)/shard_map/pallas_call | solution.py:245
  48.7 0.6 %copy.5 = f32[8,1,2,33]{3,2,1,0:T(2,128)} copy(f32[8,1,2,33]{3,0,2,1:T(8,128)S(1)} %bitcast.3) | data formatting | bytes 4224 | tf_op jit(solution)/shard_map/transpose | solution.py:276
Async XLA Ops:
  0.0 0.7 %copy-start.2 = (s32[33,3]{0,1:T(4,128)S(1)}, s32[33,3]{0,1:T(4,128)}, u32[]{:S(2)}) copy-start(s32[33,3]{0,1:T(4,128)} %param.6) | copy-start | bytes 1192
  0.7 0.7 %copy-start.1 = (s32[64,3]{0,1:T(4,128)S(1)}, s32[64,3]{0,1:T(4,128)}, u32[]{:S(2)}) copy-start(s32[64,3]{0,1:T(4,128)} %param.5) | copy-start | bytes 2308
  1.4 1.1 %copy-start = (bf16[8,2,144,128]{3,2,1,0:T(8,128)(2,1)S(1)}, bf16[8,2,144,128]{3,2,1,0:T(8,128)(2,1)}, u32[]{:S(2)}) copy-start(bf16[8,2,144,128]{3,2,1,0:T(8,128)(2,1)} %prop.1) | copy-start | bytes 1769476

commit v2 on v1

v2 whole, which is shorter than its diff:
```python
import functools
import math

import jax
import jax.numpy as jnp
from jax import lax
from jax.experimental import pallas as pl
from jax.experimental.pallas import tpu as pltpu
from jax.sharding import PartitionSpec as P

LAT = 96
NC2 = 144
K = 2 * NC2
NMOM = 33
NSRC_AX = 8
NQ = 4
NZ = 16
LANES = 128
MESH = pl.DeviceIdType.MESH
BF = jnp.bfloat16
F32 = jnp.float32


def swap_bits(vs, bits, lane):
    vs = list(vs)
    for bit, s in bits:
        low = (lane & s) == 0
        for u in range(len(vs)):
            if u & bit:
                continue
            a, b = vs[u], vs[u | bit]
            vs[u] = jnp.where(low, a, pltpu.roll(b, s, 1))
            vs[u | bit] = jnp.where(low, pltpu.roll(a, LANES - s, 1), b)
    return vs


def mod_lat(u):
    return u - LAT * jnp.floor((u + 0.5) * (1.0 / LAT))


def cos_steps(u):
    t = (jnp.abs(u - 48.0) - 24.0) * (2.0 * math.pi / LAT)
    t2 = t * t
    acc = jnp.full_like(t, 1.0 / math.factorial(13))
    for n in (11, 9, 7, 5, 3, 1):
        sign = 1.0 if n % 4 == 1 else -1.0
        acc = acc * t2 + sign / math.factorial(n)
    return acc * t


def kernel(
    prop, coords_any, momenta_any, slab_any, out,
    x_in, coords, momenta, slab, send1, recv1, lt, wg, send2, recv2, lhs, wts, send3, recv3,
    in_sem, loc_sem, s1, r1, s2, r2, s3, r3,
):
    src = lax.axis_index("src")
    space = lax.axis_index("space")
    z = space // NQ
    q = space % NQ
    sx = src % 4
    sy = src // 4

    loads = [pltpu.make_async_copy(prop.at[:, c], x_in.at[:, c], in_sem.at[c]) for c in range(2)]
    small = [
        pltpu.make_async_copy(slab_any, slab, in_sem.at[2]),
        pltpu.make_async_copy(momenta_any, momenta, in_sem.at[3]),
        pltpu.make_async_copy(coords_any, coords, in_sem.at[4]),
    ]
    for cp in loads + small:
        cp.start()

    barrier = pltpu.get_barrier_semaphore()
    for r in range(1, NSRC_AX * NQ):
        dev = {"src": (src + r // NQ) % NSRC_AX, "space": z * NQ + (q + r) % NQ}
        pl.semaphore_signal(barrier, inc=1, device_id=dev, device_id_type=MESH)
    for r in range(1, NZ):
        dev = {"src": src, "space": ((z + r) % NZ) * NQ + q}
        pl.semaphore_signal(barrier, inc=1, device_id=dev, device_id_type=MESH)

    lane16 = lax.broadcasted_iota(jnp.int32, (16, LANES), 1)
    for c in range(2):
        loads[c].wait()
        for t in range(NC2 // 16):
            vs = [x_in[b, c, t * 16 : t * 16 + 16, :] for b in range(8)]
            vs = swap_bits(vs, ((1, 1), (2, 2), (4, 4)), lane16)
            for d in range(8):
                row = c * NC2 + t * 16
                send1[d, row : row + 16, :] = vs[d]

    pl.semaphore_wait(barrier, NSRC_AX * NQ - 1 + NZ - 1)

    order = ((0, 1), (0, 3), (1, 0), (0, 2), (1, 1), (1, 3), (1, 2))
    own = pltpu.make_async_copy(send1.at[src], recv1.at[src], loc_sem.at[0])
    own.start()
    sent = []
    for dy, dx in order:
        d = ((sy + dy) % 2) * 4 + (sx + dx) % 4
        cp = pltpu.make_async_remote_copy(
            src_ref=send1.at[d], dst_ref=recv1.at[src], send_sem=s1.at[d], recv_sem=r1.at[src],
            device_id={"src": d, "space": space}, device_id_type=MESH,
        )
        cp.start()
        sent.append(cp)

    for cp in small:
        cp.wait()
    lane1 = lax.broadcasted_iota(jnp.int32, (1, LANES), 1)
    first_half = lane1 < NMOM
    m3 = momenta[...].astype(F32)
    m3 = jnp.concatenate([m3, m3, jnp.zeros((3, LANES - 2 * NMOM), F32)], axis=1)
    base = slab[0] + z * (NQ * LANES)
    shift_a = jnp.where(first_half, 0.0, 24.0)
    shift_b = jnp.where(first_half, 72.0, 0.0)
    rows = 64

    def phases(step, carry):
        row = lax.broadcasted_iota(jnp.int32, (rows, LANES), 0) + step * rows
        local = ((row >> 7) << 7) + (((row >> 5) & 3) << 1) + ((row >> 2) & 1) + (((row >> 3) & 3) << 3) + ((row & 3) << 5)
        site = local + base
        site = jnp.where(site >= LAT * LAT * LAT, site - LAT * LAT * LAT, site).astype(F32)
        x0 = jnp.floor((site + 0.5) * (1.0 / (LAT * LAT)))
        rest = site - x0 * (LAT * LAT)
        x1 = jnp.floor((rest + 0.5) * (1.0 / LAT))
        x2 = rest - x1 * LAT
        u = x0 * m3[0:1] + x1 * m3[1:2] + x2 * m3[2:3]
        w = jnp.concatenate([cos_steps(mod_lat(u + shift_a)), cos_steps(mod_lat(u + shift_b))], axis=1)
        wts[pl.ds(pl.multiple_of(step * rows, rows), rows), :] = w.astype(BF)
        return carry

    lax.fori_loop(0, NQ * LANES // rows, phases, 0)

    here = lax.broadcasted_iota(jnp.int32, (3, 64), 1) == space
    xyz = jnp.sum(jnp.where(here, coords[...].astype(F32), 0.0), axis=1, keepdims=True)
    u = jnp.sum(xyz * m3, axis=0, keepdims=True)
    scale = 1.0 / math.sqrt(NZ * NQ * LANES)
    cosine = cos_steps(mod_lat(u)) * scale
    sine = cos_steps(mod_lat(u + jnp.where(first_half, 24.0, 72.0))) * scale

    def take(j):
        turned = recv1[j].T
        for g in range(4):
            lt[g, pl.ds(pl.multiple_of(j * 32, 32), 32), :] = turned[g * 32 : g * 32 + 32]

    own.wait()
    take(src)
    for dy, dx in order:
        d = ((sy - dy + 2) % 2) * 4 + (sx - dx + 4) % 4
        pltpu.make_async_remote_copy(
            src_ref=send1.at[d], dst_ref=recv1.at[d], send_sem=s1.at[d], recv_sem=r1.at[d],
            device_id={"src": d, "space": space}, device_id_type=MESH,
        ).wait_recv()
        take(d)

    me = src * NQ + q
    lane8 = (lax.broadcasted_iota(jnp.int32, (8, LANES), 1) >> 3) & 3
    picks = [lane8 == x for x in range(4)]

    for jhi in range(2):
        for t in range(K // 16):
            at = t * 16
            vs = [recv1[4 * jhi + jlo, at : at + 16, :] for jlo in range(4)]
            vs = swap_bits(vs, ((1, 32), (2, 64)), lane16)
            for g in range(4):
                wg[g, at : at + 16, :LANES] = vs[g]
                if at < NC2:
                    wg[g, NC2 + at : NC2 + at + 16, LANES:] = -vs[g]
                else:
                    wg[g, at - NC2 : at - NC2 + 16, LANES:] = vs[g]
        traces = []
        for g in range(4):
            tt = jnp.dot(lt[g], wg[g], preferred_element_type=F32)
            for i in range(8):
                parts = []
                for c in range(2):
                    acc = tt[i * 32 : i * 32 + 8, c * LANES : (c + 1) * LANES]
                    for x in range(1, 4):
                        acc = jnp.where(picks[x], tt[i * 32 + 8 * x : i * 32 + 8 * x + 8, c * LANES : (c + 1) * LANES], acc)
                    parts.append(acc)
                traces.append(jnp.concatenate(parts, axis=0).astype(BF))
        for i in range(8):
            vs = swap_bits([traces[g * 8 + i] for g in range(4)], ((1, 1), (2, 2)), lane16)
            for t in range(4):
                send2[jhi, i * NQ + t] = vs[t]
        cp = pltpu.make_async_copy(send2.at[jhi, me], recv2.at[jhi, me], loc_sem.at[1 + jhi])
        cp.start()
        for r in range(1, NSRC_AX * NQ):
            ds, dq = (src + r // NQ) % NSRC_AX, (q + r) % NQ
            to = ds * NQ + dq
            cp = pltpu.make_async_remote_copy(
                src_ref=send2.at[jhi, to], dst_ref=recv2.at[jhi, me], send_sem=s2.at[jhi, to], recv_sem=r2.at[jhi, me],
                device_id={"src": ds, "space": z * NQ + dq}, device_id_type=MESH,
            )
            cp.start()
            sent.append(cp)

    for jhi in range(2):
        pltpu.make_async_copy(send2.at[jhi, me], recv2.at[jhi, me], loc_sem.at[1 + jhi]).wait()
        for r in range(1, NSRC_AX * NQ):
            ds, dq = (src - r // NQ + NSRC_AX) % NSRC_AX, (q - r % NQ + NQ) % NQ
            at = ds * NQ + dq
            pltpu.make_async_remote_copy(
                src_ref=send2.at[jhi, at], dst_ref=recv2.at[jhi, at], send_sem=s2.at[jhi, at], recv_sem=r2.at[jhi, at],
                device_id={"src": ds, "space": z * NQ + dq}, device_id_type=MESH,
            ).wait_recv()
        for qq in range(NQ):
            vs = [recv2[jhi, d * NQ + qq] for d in range(8)]
            vs = swap_bits(vs, ((1, 4), (2, 32), (4, 64)), lane16)
            for b in range(8):
                lhs[b * 16 : b * 16 + 16, qq * LANES : (qq + 1) * LANES] = vs[b]
        prod = jnp.dot(lhs[...], wts[...], preferred_element_type=F32)
        for b in range(8):
            send3[8 * jhi + b] = prod[b * 16 : b * 16 + 8, :LANES] + prod[b * 16 + 8 : b * 16 + 16, LANES:]
        for b in range(8):
            to = 8 * jhi + b

            @pl.when(z != to)
            def _():
                pltpu.make_async_remote_copy(
                    src_ref=send3.at[to], dst_ref=recv3.at[z], send_sem=s3.at[to], recv_sem=r3.at[z],
                    device_id={"src": src, "space": to * NQ + q}, device_id_type=MESH,
                ).start()

            @pl.when(z == to)
            def _():
                pltpu.make_async_copy(send3.at[to], recv3.at[to], loc_sem.at[3]).start()

    pltpu.make_async_copy(send3.at[z], recv3.at[z], loc_sem.at[3]).wait()
    for r in range(1, NZ):
        at = (z + r) % NZ
        cp = pltpu.make_async_remote_copy(
            src_ref=send3.at[at], dst_ref=recv3.at[at], send_sem=s3.at[at], recv_sem=r3.at[at],
            device_id={"src": src, "space": at * NQ + q}, device_id_type=MESH,
        )
        cp.wait_recv()
        sent.append(cp)
    total = recv3[0]
    for t in range(1, NZ):
        total = total + recv3[t]
    swapped = jnp.where(first_half, pltpu.roll(total, LANES - NMOM, 1), pltpu.roll(total, NMOM, 1))
    done = total * cosine + swapped * sine
    out[0, 0] = done[:, :NMOM]
    out[0, 1] = pltpu.roll(done, LANES - NMOM, 1)[:, :NMOM]

    for cp in sent:
        cp.wait_send()


def per_device(propagators, source_coords, momenta, slab_start):
    dma = pltpu.SemaphoreType.DMA
    result = pl.pallas_call(
        kernel,
        out_shape=jax.ShapeDtypeStruct((1, 2, 8, NMOM), F32),
        in_specs=[pl.BlockSpec(memory_space=pltpu.HBM)] * 4,
        out_specs=pl.BlockSpec(memory_space=pltpu.VMEM),
        scratch_shapes=[
            pltpu.VMEM((8, 2, NC2, LANES), BF),
            pltpu.VMEM((3, 64), jnp.int32),
            pltpu.VMEM((3, NMOM), jnp.int32),
            pltpu.SMEM((1,), jnp.int32),
            pltpu.VMEM((8, K, LANES), BF),
            pltpu.VMEM((8, K, LANES), BF),
            pltpu.VMEM((4, 256, K), BF),
            pltpu.VMEM((4, K, 2 * LANES), BF),
            pltpu.VMEM((2, 32, 16, LANES), BF),
            pltpu.VMEM((2, 32, 16, LANES), BF),
            pltpu.VMEM((LANES, NQ * LANES), BF),
            pltpu.VMEM((NQ * LANES, 2 * LANES), BF),
            pltpu.VMEM((NZ, 8, LANES), F32),
            pltpu.VMEM((NZ, 8, LANES), F32),
            dma((5,)),
            dma((4,)),
            dma((8,)),
            dma((8,)),
            dma((2, 32)),
            dma((2, 32)),
            dma((16,)),
            dma((16,)),
        ],
        compiler_params=pltpu.CompilerParams(
            collective_id=0, has_side_effects=True, vmem_limit_bytes=60 * 1024 * 1024
        ),
    )(propagators, source_coords.T, momenta.T, slab_start)
    return jnp.transpose(result, (2, 0, 1, 3))


def solution(mesh):
    placed = (P("src", None, None, "space"), P(), P(), P())
    return jax.shard_map(
        per_device,
        mesh=mesh,
        in_specs=placed,
        out_specs=P("src", "space", None, None),
        check_vma=False,
    )
```

time: 49.6 us -> 43.5 us (0.88)
  Pallas kernels: 46.2 us -> 41.3 us
  local copies, waits for them, and re-layouts: 2.34 us -> 1.3 us
    pallas_call x1, Pallas kernels: 46.2 us -> 41.3 us  [per_device(): pl.pallas_call(kernel, out_shape=jax.ShapeDtypeStruct((1, 2, 8, NMOM), F3...]
    unnamed x6 -> x0, local copies, waits for them, and re-layouts: 1.73 us -> none
    transpose x1, local copies, waits for them, and re-layouts: 0.6 us -> 1.3 us  [per_device(): return jnp.transpose(result, (2, 0, 1, 3))]
where the time goes in v2:
time: 43.5 us; the launch traced here: 43.3 us
  Pallas kernels  41.3 us (95%)
  local copies, waits for them, and re-layouts  1.3 us (3%)
  between operations  0.66 us (2%)
    pallas_call x1, Pallas kernels, per_device(): pl.pallas_call(kernel, out_shape=jax.ShapeDtypeStruct((1, 2, 8, NMOM), F3...  41.3 us
    transpose x1, local copies, waits for them, and re-layouts, per_device(): return jnp.transpose(result, (2, 0, 1, 3))  1.3 us

profile of v2, /device:TPU:1, one launch (start us, length us, event | category | flops | bytes accessed | tf_op | source)
XLA Modules:
  0.0 43.3 jit_solution(13587319518490941294)
XLA Ops:
  0.7 41.3 %shard_map.46 = f32[1,2,8,33]{3,2,1,0:T(8,128)} custom-call(bf16[8,2,144,128]{3,2,1,0:T(8,128)(2,1)} %prop.1, s32[3,64]{1,0:T(4,128)} %bitcast.4, s32[3,33]{1,0:T(4,128)} %bitcast.5, s32[1]{0:T(128)S(6)} %copy.6.slab_any), custom_call_target="tpu_custom_call" | custom-call | tf_op jit(solution)/shard_map/pallas_call | solution.py:250
  42.0 1.3 %copy.5 = f32[8,1,2,33]{3,2,1,0:T(2,128)} copy(f32[8,1,2,33]{3,0,2,1:T(8,128)} %bitcast.3) | data formatting | bytes 4224 | tf_op jit(solution)/shard_map/transpose | solution.py:283

commit v3 on v2

--- a/solution.py
+++ b/solution.py
@@ -49,9 +49,9 @@
 
 
 def kernel(
-    prop, coords_any, momenta_any, slab_any, out,
-    x_in, coords, momenta, slab, send1, recv1, lt, wg, send2, recv2, lhs, wts, send3, recv3,
-    in_sem, loc_sem, s1, r1, s2, r2, s3, r3,
+    prop, coords_any, momenta_any, slab, out,
+    x_in, coords, momenta, send1, recv1, lt, wg, send2, recv2, lhs, wts, send3, recv3,
+    in_sem, loc_sem, s1, r1, s2, r2, s3, r3, known,
 ):
     src = lax.axis_index("src")
     space = lax.axis_index("space")
@@ -62,20 +62,22 @@
 
     loads = [pltpu.make_async_copy(prop.at[:, c], x_in.at[:, c], in_sem.at[c]) for c in range(2)]
     small = [
-        pltpu.make_async_copy(slab_any, slab, in_sem.at[2]),
         pltpu.make_async_copy(momenta_any, momenta, in_sem.at[3]),
         pltpu.make_async_copy(coords_any, coords, in_sem.at[4]),
     ]
+    barrier = pltpu.get_barrier_semaphore()
+    z_mates = [{"src": src, "space": ((z + r) % NZ) * NQ + q} for r in (1, NZ - 1, 2, NZ - 2, 4, NZ - 4)]
+    q_mates = [{"src": src, "space": z * NQ + (q + r) % NQ} for r in range(1, NQ)]
+    src_mates = [{"src": (src + r) % NSRC_AX, "space": space} for r in range(1, NSRC_AX)]
+    first = src_mates + q_mates + z_mates[:2]
+    for dev in first:
+        pl.semaphore_signal(barrier, inc=1, device_id=dev, device_id_type=MESH)
     for cp in loads + small:
         cp.start()
 
-    barrier = pltpu.get_barrier_semaphore()
-    for r in range(1, NSRC_AX * NQ):
-        dev = {"src": (src + r // NQ) % NSRC_AX, "space": z * NQ + (q + r) % NQ}
-        pl.semaphore_signal(barrier, inc=1, device_id=dev, device_id_type=MESH)
-    for r in range(1, NZ):
-        dev = {"src": src, "space": ((z + r) % NZ) * NQ + q}
-        pl.semaphore_signal(barrier, inc=1, device_id=dev, device_id_type=MESH)
+    def tell(level, devs):
+        for dev in devs:
+            pl.semaphore_signal(known.at[level], inc=1, device_id=dev, device_id_type=MESH)
 
     lane16 = lax.broadcasted_iota(jnp.int32, (16, LANES), 1)
     for c in range(2):
@@ -87,9 +89,9 @@
                 row = c * NC2 + t * 16
                 send1[d, row : row + 16, :] = vs[d]
 
-    pl.semaphore_wait(barrier, NSRC_AX * NQ - 1 + NZ - 1)
-
-    order = ((0, 1), (0, 3), (1, 0), (0, 2), (1, 1), (1, 3), (1, 2))
+    pl.semaphore_wait(barrier, len(first))
+
+    order = ((1, 2), (1, 1), (1, 3), (0, 2), (1, 0), (0, 1), (0, 3))
     own = pltpu.make_async_copy(send1.at[src], recv1.at[src], loc_sem.at[0])
     own.start()
     sent = []
@@ -101,6 +103,9 @@
         )
         cp.start()
         sent.append(cp)
+
+    tell(0, q_mates)
+    tell(1, z_mates[:2])
 
     for cp in small:
         cp.wait()
@@ -143,7 +148,10 @@
 
     own.wait()
     take(src)
-    for dy, dx in order:
+    for n, (dy, dx) in enumerate(reversed(order)):
+        if n == 3:
+            pl.semaphore_wait(known.at[1], 2)
+            tell(2, z_mates[2:4])
         d = ((sy - dy + 2) % 2) * 4 + (sx - dx + 4) % 4
         pltpu.make_async_remote_copy(
             src_ref=send1.at[d], dst_ref=recv1.at[d], send_sem=s1.at[d], recv_sem=r1.at[d],
@@ -152,6 +160,14 @@
         take(d)
 
     me = src * NQ + q
+    y = 2 * sy + q // 2
+
+    def mate(dx, dy, dc):
+        at = (y + dy) % 4
+        return (at // 2) * 4 + (sx + dx) % 4, (at % 2) * 2 + (q + dc) % 2
+
+    hops = [(dx, dy, dc) for dx in range(4) for dy in range(4) for dc in range(2) if dx + dy + dc]
+    hops.sort(key=lambda h: -min(h[0], 4 - h[0]) - min(h[1], 4 - h[1]))
     lane8 = (lax.broadcasted_iota(jnp.int32, (8, LANES), 1) >> 3) & 3
     picks = [lane8 == x for x in range(4)]
 
@@ -181,10 +197,10 @@
             vs = swap_bits([traces[g * 8 + i] for g in range(4)], ((1, 1), (2, 2)), lane16)
             for t in range(4):
                 send2[jhi, i * NQ + t] = vs[t]
-        cp = pltpu.make_async_copy(send2.at[jhi, me], recv2.at[jhi, me], loc_sem.at[1 + jhi])
-        cp.start()
-        for r in range(1, NSRC_AX * NQ):
-            ds, dq = (src + r // NQ) % NSRC_AX, (q + r) % NQ
+        if jhi == 0:
+            pl.semaphore_wait(known.at[0], NQ - 1)
+        for dx, dy, dc in hops:
+            ds, dq = mate(dx, dy, dc)
             to = ds * NQ + dq
             cp = pltpu.make_async_remote_copy(
                 src_ref=send2.at[jhi, to], dst_ref=recv2.at[jhi, me], send_sem=s2.at[jhi, to], recv_sem=r2.at[jhi, me],
@@ -192,11 +208,15 @@
             )
             cp.start()
             sent.append(cp)
+        pltpu.make_async_copy(send2.at[jhi, me], recv2.at[jhi, me], loc_sem.at[1 + jhi]).start()
+        if jhi == 0:
+            pl.semaphore_wait(known.at[2], 2)
+            tell(3, z_mates[4:])
 
     for jhi in range(2):
         pltpu.make_async_copy(send2.at[jhi, me], recv2.at[jhi, me], loc_sem.at[1 + jhi]).wait()
-        for r in range(1, NSRC_AX * NQ):
-            ds, dq = (src - r // NQ + NSRC_AX) % NSRC_AX, (q - r % NQ + NQ) % NQ
+        for dx, dy, dc in reversed(hops):
+            ds, dq = mate(dx, dy, dc)
             at = ds * NQ + dq
             pltpu.make_async_remote_copy(
                 src_ref=send2.at[jhi, at], dst_ref=recv2.at[jhi, at], send_sem=s2.at[jhi, at], recv_sem=r2.at[jhi, at],
@@ -210,6 +230,8 @@
         prod = jnp.dot(lhs[...], wts[...], preferred_element_type=F32)
         for b in range(8):
             send3[8 * jhi + b] = prod[b * 16 : b * 16 + 8, :LANES] + prod[b * 16 + 8 : b * 16 + 16, LANES:]
+        if jhi == 0:
+            pl.semaphore_wait(known.at[3], 2)
         for b in range(8):
             to = 8 * jhi + b
 
@@ -224,7 +246,11 @@
             def _():
                 pltpu.make_async_copy(send3.at[to], recv3.at[to], loc_sem.at[3]).start()
 
+    for cp in sent:
+        cp.wait_send()
+
     pltpu.make_async_copy(send3.at[z], recv3.at[z], loc_sem.at[3]).wait()
+    last = []
     for r in range(1, NZ):
         at = (z + r) % NZ
         cp = pltpu.make_async_remote_copy(
@@ -232,31 +258,29 @@
             device_id={"src": src, "space": at * NQ + q}, device_id_type=MESH,
         )
         cp.wait_recv()
-        sent.append(cp)
+        last.append(cp)
     total = recv3[0]
     for t in range(1, NZ):
         total = total + recv3[t]
     swapped = jnp.where(first_half, pltpu.roll(total, LANES - NMOM, 1), pltpu.roll(total, NMOM, 1))
     done = total * cosine + swapped * sine
-    out[0, 0] = done[:, :NMOM]
-    out[0, 1] = pltpu.roll(done, LANES - NMOM, 1)[:, :NMOM]
-
-    for cp in sent:
+    out[:, 0, 0] = done[:, :NMOM]
+    out[:, 0, 1] = pltpu.roll(done, LANES - NMOM, 1)[:, :NMOM]
+    for cp in last:
         cp.wait_send()
 
 
 def per_device(propagators, source_coords, momenta, slab_start):
     dma = pltpu.SemaphoreType.DMA
-    result = pl.pallas_call(
+    return pl.pallas_call(
         kernel,
-        out_shape=jax.ShapeDtypeStruct((1, 2, 8, NMOM), F32),
-        in_specs=[pl.BlockSpec(memory_space=pltpu.HBM)] * 4,
+        out_shape=pltpu.VMEM((8, 1, 2, NMOM), F32),
+        in_specs=[pl.BlockSpec(memory_space=pltpu.HBM)] * 3 + [pl.BlockSpec(memory_space=pltpu.SMEM)],
         out_specs=pl.BlockSpec(memory_space=pltpu.VMEM),
         scratch_shapes=[
             pltpu.VMEM((8, 2, NC2, LANES), BF),
             pltpu.VMEM((3, 64), jnp.int32),
             pltpu.VMEM((3, NMOM), jnp.int32),
-            pltpu.SMEM((1,), jnp.int32),
             pltpu.VMEM((8, K, LANES), BF),
             pltpu.VMEM((8, K, LANES), BF),
             pltpu.VMEM((4, 256, K), BF),
@@ -275,12 +299,12 @@
             dma((2, 32)),
             dma((16,)),
             dma((16,)),
+            pltpu.SemaphoreType.REGULAR((4,)),
         ],
         compiler_params=pltpu.CompilerParams(
-            collective_id=0, has_side_effects=True, vmem_limit_bytes=60 * 1024 * 1024
+            collective_id=0, has_side_effects=True, vmem_limit_bytes=32 * 1024 * 1024
         ),
-    )(propagators, source_coords.T, momenta.T, slab_start)
-    return jnp.transpose(result, (2, 0, 1, 3))
+    )(*[pltpu.with_memory_space_constraint(x, pltpu.HBM) for x in (propagators, source_coords.T, momenta.T)], slab_start)
 
 
 def solution(mesh):

time: 43.5 us -> 40.2 us (0.924)
  Pallas kernels: 41.3 us -> 38.8 us
  local copies, waits for them, and re-layouts: 1.3 us -> 0.6 us
    pallas_call x1, Pallas kernels: 41.3 us -> 38.8 us  [per_device(): pl.pallas_call(kernel, out_shape=pltpu.VMEM((8, 1, 2, NMOM), F32), in_spe...]
    transpose x1 -> x0, local copies, waits for them, and re-layouts: 1.3 us -> none  [per_device(): return jnp.transpose(result, (2, 0, 1, 3))]
    unnamed x0 -> x1, local copies, waits for them, and re-layouts: none -> 0.6 us
where the time goes in v3:
time: 40.2 us; the launch traced here: 40 us
  Pallas kernels  38.8 us (97%)
  between operations  0.66 us (2%)
  local copies, waits for them, and re-layouts  0.6 us (1%)
    pallas_call x1, Pallas kernels, per_device(): pl.pallas_call(kernel, out_shape=pltpu.VMEM((8, 1, 2, NMOM), F32), in_spe...  38.8 us

profile of v3, /device:TPU:1, one launch (start us, length us, event | category | flops | bytes accessed | tf_op | source)
XLA Modules:
  0.0 40.0 jit_solution(10714118271838297775)
XLA Ops:
  0.7 38.8 %shard_map.46 = f32[8,1,2,33]{3,2,1,0:T(2,128)S(1)} custom-call(bf16[8,2,144,128]{3,2,1,0:T(8,128)(2,1)} %prop.1, s32[3,64]{1,0:T(4,128)} %bitcast.2, s32[3,33]{1,0:T(4,128)} %bitcast.3, s32[1]{0:T(128)S(6)} %copy.7.slab), custom_call_target="tpu_custom_call" | custom-call | tf_op jit(solution)/shard_map/pallas_call | solution.py:275
  39.4 0.6 %copy.6 = f32[8,1,2,33]{3,2,1,0:T(2,128)} copy(f32[8,1,2,33]{3,2,1,0:T(2,128)S(1)} %shard_map.46) | data formatting | bytes 4224

commit v4 on v3

--- a/solution.py
+++ b/solution.py
@@ -68,8 +68,9 @@
     barrier = pltpu.get_barrier_semaphore()
     z_mates = [{"src": src, "space": ((z + r) % NZ) * NQ + q} for r in (1, NZ - 1, 2, NZ - 2, 4, NZ - 4)]
     q_mates = [{"src": src, "space": z * NQ + (q + r) % NQ} for r in range(1, NQ)]
-    src_mates = [{"src": (src + r) % NSRC_AX, "space": space} for r in range(1, NSRC_AX)]
-    first = src_mates + q_mates + z_mates[:2]
+    order = ((1, 2), (1, 1), (1, 3), (0, 2), (1, 0), (0, 1), (0, 3))
+    src_mates = [{"src": ((sy + dy) % 2) * 4 + (sx + dx) % 4, "space": space} for dy, dx in order]
+    first = src_mates + z_mates[:2] + q_mates
     for dev in first:
         pl.semaphore_signal(barrier, inc=1, device_id=dev, device_id_type=MESH)
     for cp in loads + small:
@@ -91,7 +92,6 @@
 
     pl.semaphore_wait(barrier, len(first))
 
-    order = ((1, 2), (1, 1), (1, 3), (0, 2), (1, 0), (0, 1), (0, 3))
     own = pltpu.make_async_copy(send1.at[src], recv1.at[src], loc_sem.at[0])
     own.start()
     sent = []
@@ -148,10 +148,13 @@
 
     own.wait()
     take(src)
-    for n, (dy, dx) in enumerate(reversed(order)):
-        if n == 3:
+    for n, (dy, dx) in enumerate(order):
+        if n == 0:
             pl.semaphore_wait(known.at[1], 2)
             tell(2, z_mates[2:4])
+        if n == 3:
+            pl.semaphore_wait(known.at[2], 2)
+            tell(3, z_mates[4:])
         d = ((sy - dy + 2) % 2) * 4 + (sx - dx + 4) % 4
         pltpu.make_async_remote_copy(
             src_ref=send1.at[d], dst_ref=recv1.at[d], send_sem=s1.at[d], recv_sem=r1.at[d],
@@ -170,6 +173,27 @@
     hops.sort(key=lambda h: -min(h[0], 4 - h[0]) - min(h[1], 4 - h[1]))
     lane8 = (lax.broadcasted_iota(jnp.int32, (8, LANES), 1) >> 3) & 3
     picks = [lane8 == x for x in range(4)]
+
+    def send_traces(jhi):
+        for dx, dy, dc in hops:
+            ds, dq = mate(dx, dy, dc)
+            to = ds * NQ + dq
+            cp = pltpu.make_async_remote_copy(
+                src_ref=send2.at[jhi, to], dst_ref=recv2.at[jhi, me], send_sem=s2.at[jhi, to], recv_sem=r2.at[jhi, me],
+                device_id={"src": ds, "space": z * NQ + dq}, device_id_type=MESH,
+            )
+            cp.start()
+            sent.append(cp)
+        pltpu.make_async_copy(send2.at[jhi, me], recv2.at[jhi, me], loc_sem.at[1 + jhi]).start()
+
+    def traces_here(jhi, some):
+        for dx, dy, dc in some:
+            ds, dq = mate(dx, dy, dc)
+            at = ds * NQ + dq
+            pltpu.make_async_remote_copy(
+                src_ref=send2.at[jhi, at], dst_ref=recv2.at[jhi, at], send_sem=s2.at[jhi, at], recv_sem=r2.at[jhi, at],
+                device_id={"src": ds, "space": z * NQ + dq}, device_id_type=MESH,
+            ).wait_recv()
 
     for jhi in range(2):
         for t in range(K // 16):
@@ -199,29 +223,17 @@
                 send2[jhi, i * NQ + t] = vs[t]
         if jhi == 0:
             pl.semaphore_wait(known.at[0], NQ - 1)
-        for dx, dy, dc in hops:
-            ds, dq = mate(dx, dy, dc)
-            to = ds * NQ + dq
-            cp = pltpu.make_async_remote_copy(
-                src_ref=send2.at[jhi, to], dst_ref=recv2.at[jhi, me], send_sem=s2.at[jhi, to], recv_sem=r2.at[jhi, me],
-                device_id={"src": ds, "space": z * NQ + dq}, device_id_type=MESH,
-            )
-            cp.start()
-            sent.append(cp)
-        pltpu.make_async_copy(send2.at[jhi, me], recv2.at[jhi, me], loc_sem.at[1 + jhi]).start()
-        if jhi == 0:
-            pl.semaphore_wait(known.at[2], 2)
-            tell(3, z_mates[4:])
+            send_traces(0)
 
     for jhi in range(2):
         pltpu.make_async_copy(send2.at[jhi, me], recv2.at[jhi, me], loc_sem.at[1 + jhi]).wait()
-        for dx, dy, dc in reversed(hops):
-            ds, dq = mate(dx, dy, dc)
-            at = ds * NQ + dq
-            pltpu.make_async_remote_copy(
-                src_ref=send2.at[jhi, at], dst_ref=recv2.at[jhi, at], send_sem=s2.at[jhi, at], recv_sem=r2.at[jhi, at],
-                device_id={"src": ds, "space": z * NQ + dq}, device_id_type=MESH,
-            ).wait_recv()
+        near_first = hops[::-1]
+        if jhi == 0:
+            traces_here(0, near_first[:1])
+            send_traces(1)
+            traces_here(0, near_first[1:])
+        else:
+            traces_here(1, near_first)
         for qq in range(NQ):
             vs = [recv2[jhi, d * NQ + qq] for d in range(8)]
             vs = swap_bits(vs, ((1, 4), (2, 32), (4, 64)), lane16)
@@ -257,8 +269,11 @@
             src_ref=send3.at[at], dst_ref=recv3.at[at], send_sem=s3.at[at], recv_sem=r3.at[at],
             device_id={"src": src, "space": at * NQ + q}, device_id_type=MESH,
         )
+        last.append(cp)
+    for cp in last:
+        cp.wait_send()
+    for cp in last:
         cp.wait_recv()
-        last.append(cp)
     total = recv3[0]
     for t in range(1, NZ):
         total = total + recv3[t]
@@ -266,8 +281,6 @@
     done = total * cosine + swapped * sine
     out[:, 0, 0] = done[:, :NMOM]
     out[:, 0, 1] = pltpu.roll(done, LANES - NMOM, 1)[:, :NMOM]
-    for cp in last:
-        cp.wait_send()
 
 
 def per_device(propagators, source_coords, momenta, slab_start):

time: 40.2 us -> 39.4 us (0.980)
  Pallas kernels: 38.8 us -> 38 us
    pallas_call x1, Pallas kernels: 38.8 us -> 38 us  [per_device(): pl.pallas_call(kernel, out_shape=pltpu.VMEM((8, 1, 2, NMOM), F32), in_spe...]
where the time goes in v4:
time: 39.4 us; the launch traced here: 39.3 us
  Pallas kernels  38 us (96%)
  between operations  0.66 us (2%)
  local copies, waits for them, and re-layouts  0.6 us (2%)
    pallas_call x1, Pallas kernels, per_device(): pl.pallas_call(kernel, out_shape=pltpu.VMEM((8, 1, 2, NMOM), F32), in_spe...  38 us

profile of v4, /device:TPU:1, one launch (start us, length us, event | category | flops | bytes accessed | tf_op | source)
XLA Modules:
  0.0 39.3 jit_solution(2436278740873754085)
XLA Ops:
  0.7 38.0 %shard_map.46 = f32[8,1,2,33]{3,2,1,0:T(2,128)S(1)} custom-call(bf16[8,2,144,128]{3,2,1,0:T(8,128)(2,1)} %prop.1, s32[3,64]{1,0:T(4,128)} %bitcast.2, s32[3,33]{1,0:T(4,128)} %bitcast.3, s32[1]{0:T(128)S(6)} %copy.7.slab), custom_call_target="tpu_custom_call" | custom-call | tf_op jit(solution)/shard_map/pallas_call | solution.py:288
  38.7 0.6 %copy.6 = f32[8,1,2,33]{3,2,1,0:T(2,128)} copy(f32[8,1,2,33]{3,2,1,0:T(2,128)S(1)} %shard_map.46) | data formatting | bytes 4224

commit v5 on v4

--- a/solution.py
+++ b/solution.py
@@ -50,7 +50,7 @@
 
 def kernel(
     prop, coords_any, momenta_any, slab, out,
-    x_in, coords, momenta, send1, recv1, lt, wg, send2, recv2, lhs, wts, send3, recv3,
+    x_in, coords, momenta, mid, send1, recv1, send2, recv2, lhs, wts, send3, recv3,
     in_sem, loc_sem, s1, r1, s2, r2, s3, r3, known,
 ):
     src = lax.axis_index("src")
@@ -88,7 +88,18 @@
             vs = swap_bits(vs, ((1, 1), (2, 2), (4, 4)), lane16)
             for d in range(8):
                 row = c * NC2 + t * 16
-                send1[d, row : row + 16, :] = vs[d]
+                mid[d, row : row + 16, :] = vs[d]
+
+    def turn(d, carry):
+        block = mid[d]
+        send1[d, :LANES] = block[:LANES].T
+        send1[d, LANES : 2 * LANES] = block[NC2 : NC2 + LANES].T
+        rest = jnp.concatenate([block[LANES:NC2], block[NC2 + LANES :]], axis=0)
+        rest = jnp.concatenate([rest] + [pltpu.roll(rest, LANES - 32 * g, 1) for g in (1, 2, 3)], axis=0)
+        send1[d, 2 * LANES :] = rest.T[:32]
+        return carry
+
+    lax.fori_loop(0, NSRC_AX, turn, 0)
 
     pl.semaphore_wait(barrier, len(first))
 
@@ -141,13 +152,7 @@
     cosine = cos_steps(mod_lat(u)) * scale
     sine = cos_steps(mod_lat(u + jnp.where(first_half, 24.0, 72.0))) * scale
 
-    def take(j):
-        turned = recv1[j].T
-        for g in range(4):
-            lt[g, pl.ds(pl.multiple_of(j * 32, 32), 32), :] = turned[g * 32 : g * 32 + 32]
-
     own.wait()
-    take(src)
     for n, (dy, dx) in enumerate(order):
         if n == 0:
             pl.semaphore_wait(known.at[1], 2)
@@ -160,7 +165,6 @@
             src_ref=send1.at[d], dst_ref=recv1.at[d], send_sem=s1.at[d], recv_sem=r1.at[d],
             device_id={"src": d, "space": space}, device_id_type=MESH,
         ).wait_recv()
-        take(d)
 
     me = src * NQ + q
     y = 2 * sy + q // 2
@@ -173,6 +177,8 @@
     hops.sort(key=lambda h: -min(h[0], 4 - h[0]) - min(h[1], 4 - h[1]))
     lane8 = (lax.broadcasted_iota(jnp.int32, (8, LANES), 1) >> 3) & 3
     picks = [lane8 == x for x in range(4)]
+    lane_l = lax.broadcasted_iota(jnp.int32, (2 * LANES, LANES), 1)
+    lane_r = lax.broadcasted_iota(jnp.int32, (LANES, LANES), 1)
 
     def send_traces(jhi):
         for dx, dy, dc in hops:
@@ -196,19 +202,22 @@
             ).wait_recv()
 
     for jhi in range(2):
-        for t in range(K // 16):
-            at = t * 16
-            vs = [recv1[4 * jhi + jlo, at : at + 16, :] for jlo in range(4)]
-            vs = swap_bits(vs, ((1, 32), (2, 64)), lane16)
-            for g in range(4):
-                wg[g, at : at + 16, :LANES] = vs[g]
-                if at < NC2:
-                    wg[g, NC2 + at : NC2 + at + 16, LANES:] = -vs[g]
-                else:
-                    wg[g, at - NC2 : at - NC2 + 16, LANES:] = vs[g]
         traces = []
         for g in range(4):
-            tt = jnp.dot(lt[g], wg[g], preferred_element_type=F32)
+            def rows_of(blocks, part):
+                at = part * LANES + (32 * g if part < 2 else 0)
+                return jnp.concatenate([recv1[k, at : at + 32, :] for k in blocks], axis=0)
+
+            left = [rows_of(range(8), part) for part in range(3)]
+            left[2] = jnp.where((lane_l >> 5) == g, left[2], jnp.zeros_like(left[2]))
+            b0, b1, b2 = [rows_of(range(4 * jhi, 4 * jhi + 4), part) for part in range(3)]
+            b2t = jnp.where((lane_r & 16) == 0, pltpu.roll(b2, LANES - 16, 1), -pltpu.roll(b2, 16, 1))
+            right = jnp.concatenate(
+                [jnp.concatenate([b0, b1, b2], axis=1), jnp.concatenate([b1, -b0, b2t], axis=1)], axis=0
+            )
+            tt = lax.dot_general(
+                jnp.concatenate(left, axis=1), right, (((1,), (1,)), ((), ())), preferred_element_type=F32
+            )
             for i in range(8):
                 parts = []
                 for c in range(2):
@@ -229,9 +238,9 @@
         pltpu.make_async_copy(send2.at[jhi, me], recv2.at[jhi, me], loc_sem.at[1 + jhi]).wait()
         near_first = hops[::-1]
         if jhi == 0:
-            traces_here(0, near_first[:1])
+            traces_here(0, near_first[:3])
             send_traces(1)
-            traces_here(0, near_first[1:])
+            traces_here(0, near_first[3:])
         else:
             traces_here(1, near_first)
         for qq in range(NQ):
@@ -296,8 +305,7 @@
             pltpu.VMEM((3, NMOM), jnp.int32),
             pltpu.VMEM((8, K, LANES), BF),
             pltpu.VMEM((8, K, LANES), BF),
-            pltpu.VMEM((4, 256, K), BF),
-            pltpu.VMEM((4, K, 2 * LANES), BF),
+            pltpu.VMEM((8, K, LANES), BF),
             pltpu.VMEM((2, 32, 16, LANES), BF),
             pltpu.VMEM((2, 32, 16, LANES), BF),
             pltpu.VMEM((LANES, NQ * LANES), BF),

time: 39.4 us -> 39.4 us (level)
  no operation moved by 1% of the time
where the time goes in v5:
time: 39.4 us; the launch traced here: 39.3 us
  Pallas kernels  38 us (96%)
  between operations  0.66 us (2%)
  local copies, waits for them, and re-layouts  0.6 us (2%)
    pallas_call x1, Pallas kernels, per_device(): pl.pallas_call(kernel, out_shape=pltpu.VMEM((8, 1, 2, NMOM), F32), in_spe...  38 us

profile of v5, /device:TPU:1, one launch (start us, length us, event | category | flops | bytes accessed | tf_op | source)
XLA Modules:
  0.0 39.3 jit_solution(3351231768709716948)
XLA Ops:
  0.7 38.0 %shard_map.46 = f32[8,1,2,33]{3,2,1,0:T(2,128)S(1)} custom-call(bf16[8,2,144,128]{3,2,1,0:T(8,128)(2,1)} %prop.1, s32[3,64]{1,0:T(4,128)} %bitcast.2, s32[3,33]{1,0:T(4,128)} %bitcast.3, s32[1]{0:T(128)S(6)} %copy.7.slab), custom_call_target="tpu_custom_call" | custom-call | tf_op jit(solution)/shard_map/pallas_call | solution.py:297
  38.7 0.6 %copy.6 = f32[8,1,2,33]{3,2,1,0:T(2,128)} copy(f32[8,1,2,33]{3,2,1,0:T(2,128)S(1)} %shard_map.46) | data formatting | bytes 4224

commit v6 on v5

--- a/solution.py
+++ b/solution.py
@@ -90,30 +90,32 @@
                 row = c * NC2 + t * 16
                 mid[d, row : row + 16, :] = vs[d]
 
-    def turn(d, carry):
+    def turn(d, into):
         block = mid[d]
-        send1[d, :LANES] = block[:LANES].T
-        send1[d, LANES : 2 * LANES] = block[NC2 : NC2 + LANES].T
+        into[d, :LANES] = block[:LANES].T
+        into[d, LANES : 2 * LANES] = block[NC2 : NC2 + LANES].T
         rest = jnp.concatenate([block[LANES:NC2], block[NC2 + LANES :]], axis=0)
         rest = jnp.concatenate([rest] + [pltpu.roll(rest, LANES - 32 * g, 1) for g in (1, 2, 3)], axis=0)
-        send1[d, 2 * LANES :] = rest.T[:32]
-        return carry
-
-    lax.fori_loop(0, NSRC_AX, turn, 0)
+        into[d, 2 * LANES :] = rest.T[:32]
+
+    for dy, dx in order[:3]:
+        turn(((sy + dy) % 2) * 4 + (sx + dx) % 4, send1)
 
     pl.semaphore_wait(barrier, len(first))
 
-    own = pltpu.make_async_copy(send1.at[src], recv1.at[src], loc_sem.at[0])
-    own.start()
     sent = []
-    for dy, dx in order:
+    for n, (dy, dx) in enumerate(order):
         d = ((sy + dy) % 2) * 4 + (sx + dx) % 4
+        if n >= 3:
+            turn(d, send1)
         cp = pltpu.make_async_remote_copy(
             src_ref=send1.at[d], dst_ref=recv1.at[src], send_sem=s1.at[d], recv_sem=r1.at[src],
             device_id={"src": d, "space": space}, device_id_type=MESH,
         )
         cp.start()
         sent.append(cp)
+
+    turn(src, recv1)
 
     tell(0, q_mates)
     tell(1, z_mates[:2])
@@ -152,7 +154,6 @@
     cosine = cos_steps(mod_lat(u)) * scale
     sine = cos_steps(mod_lat(u + jnp.where(first_half, 24.0, 72.0))) * scale
 
-    own.wait()
     for n, (dy, dx) in enumerate(order):
         if n == 0:
             pl.semaphore_wait(known.at[1], 2)

time: 39.4 us -> 39.2 us (level)
  no operation moved by 1% of the time
where the time goes in v6:
time: 39.2 us; the launch traced here: 39 us
  Pallas kernels  37.8 us (96%)
  between operations  0.66 us (2%)
  local copies, waits for them, and re-layouts  0.6 us (2%)
    pallas_call x1, Pallas kernels, per_device(): pl.pallas_call(kernel, out_shape=pltpu.VMEM((8, 1, 2, NMOM), F32), in_spe...  37.8 us

profile of v6, /device:TPU:1, one launch (start us, length us, event | category | flops | bytes accessed | tf_op | source)
XLA Modules:
  0.0 39.0 jit_solution(8402753237164752643)
XLA Ops:
  0.7 37.8 %shard_map.46 = f32[8,1,2,33]{3,2,1,0:T(2,128)S(1)} custom-call(bf16[8,2,144,128]{3,2,1,0:T(8,128)(2,1)} %prop.1, s32[3,64]{1,0:T(4,128)} %bitcast.2, s32[3,33]{1,0:T(4,128)} %bitcast.3, s32[1]{0:T(128)S(6)} %copy.7.slab), custom_call_target="tpu_custom_call" | custom-call | tf_op jit(solution)/shard_map/pallas_call | solution.py:298
  38.4 0.6 %copy.6 = f32[8,1,2,33]{3,2,1,0:T(2,128)} copy(f32[8,1,2,33]{3,2,1,0:T(2,128)S(1)} %shard_map.46) | data formatting | bytes 4224

commit v7 on v6

--- a/solution.py
+++ b/solution.py
@@ -98,7 +98,7 @@
         rest = jnp.concatenate([rest] + [pltpu.roll(rest, LANES - 32 * g, 1) for g in (1, 2, 3)], axis=0)
         into[d, 2 * LANES :] = rest.T[:32]
 
-    for dy, dx in order[:3]:
+    for dy, dx in order[:1]:
         turn(((sy + dy) % 2) * 4 + (sx + dx) % 4, send1)
 
     pl.semaphore_wait(barrier, len(first))
@@ -106,7 +106,7 @@
     sent = []
     for n, (dy, dx) in enumerate(order):
         d = ((sy + dy) % 2) * 4 + (sx + dx) % 4
-        if n >= 3:
+        if n >= 1:
             turn(d, send1)
         cp = pltpu.make_async_remote_copy(
             src_ref=send1.at[d], dst_ref=recv1.at[src], send_sem=s1.at[d], recv_sem=r1.at[src],

time: 39.2 us -> 39.4 us (level)
  no operation moved by 1% of the time
where the time goes in v7:
time: 39.4 us; the launch traced here: 39.3 us
  Pallas kernels  38 us (96%)
  between operations  0.66 us (2%)
  local copies, waits for them, and re-layouts  0.6 us (2%)
    pallas_call x1, Pallas kernels, per_device(): pl.pallas_call(kernel, out_shape=pltpu.VMEM((8, 1, 2, NMOM), F32), in_spe...  38 us

profile of v7, /device:TPU:1, one launch (start us, length us, event | category | flops | bytes accessed | tf_op | source)
XLA Modules:
  0.0 39.3 jit_solution(17327109335434399504)
XLA Ops:
  0.7 38.0 %shard_map.46 = f32[8,1,2,33]{3,2,1,0:T(2,128)S(1)} custom-call(bf16[8,2,144,128]{3,2,1,0:T(8,128)(2,1)} %prop.1, s32[3,64]{1,0:T(4,128)} %bitcast.2, s32[3,33]{1,0:T(4,128)} %bitcast.3, s32[1]{0:T(128)S(6)} %copy.7.slab), custom_call_target="tpu_custom_call" | custom-call | tf_op jit(solution)/shard_map/pallas_call | solution.py:298
  38.7 0.6 %copy.6 = f32[8,1,2,33]{3,2,1,0:T(2,128)} copy(f32[8,1,2,33]{3,2,1,0:T(2,128)S(1)} %shard_map.46) | data formatting | bytes 4224
